TPU v7x, 32 devices: a whole 2x2x4 slice. The times are simulated.
32 devices in a mesh: rows: 4 (over z), cols: 2 (over y), layers: 4 (over x, core).
Axes of the slice: x: 2, y: 2, z: 4, core: 2. Of those that a mesh axis runs over, the one named last changes fastest.
Arguments:
- bottom_known_vector: float32 [192, 128, 256], P(('rows', 'layers')), may hold values from -6 to 6
- bottom_pivot_reciprocal: float32 [192, 128, 128], P(('rows', 'layers'), 'cols'), as said below
- leaf_blocks: float32 [192, 2, 128, 128], P(('rows', 'layers'), 'cols'), may hold values from -0.0546875 to 0.0546875
- leaf_target: int32 [192, 2], P(('rows', 'layers'), 'cols'), may hold values from 0 to 3, as said below
- top_rhs: float32 [4, 128, 256], P('rows'), may hold values from -6 to 6
- top_inv: float32 [4, 128, 128], P('rows'), as said below
- top_sub: float32 [4, 128, 128], P('rows'), may hold values from -0.4375 to 0.4375
Outputs:
- leaf_solution: float32 [192, 128, 256], P(('rows', 'layers'), 'cols')
- top_solution: float32 [4, 128, 256], P('rows')
Inputs may be any that keep to these rules, and one draw needn't show every extreme that they name: `leaf_target`: each leaf names 2 different top supernodes. `bottom_pivot_reciprocal`: each block is its diagonal times a factor of 0.7 to 1.3 plus a full-rank off-diagonal part. `top_inv`: each block is its diagonal times a factor of 0.7 to 1.3 plus a full-rank off-diagonal part.
All inputs are finite; a program needn't handle non-finite values.
Results may differ from a plain program's by a relative error of at most 0.00028.
Values sent between devices are 32-bit elements; how exact they have to be, the bound alone decides.
A program may use at most 64 MiB of HBM per device.

v0:
```python
import jax
import jax.numpy as jnp
from jax import lax
from jax.sharding import PartitionSpec as P


def from_behind(x, axis, by):
    peers = lax.axis_size(axis)
    pairs = [(i, i + by) for i in range(peers) if 0 <= i + by < peers]
    return lax.ppermute(x, axis, pairs)


def on_device(
    bottom_known_vector,
    bottom_pivot_reciprocal,
    leaf_blocks,
    leaf_target,
    top_rhs,
    top_inv,
    top_sub,
):
    exact_arithmetic_mode = lax.Precision.HIGHEST
    row_count = lax.axis_size("rows")
    distribute_equations = bottom_pivot_reciprocal.shape[1]
    forward_portion = jnp.einsum(
        "bxr,brl->bxl",
        bottom_pivot_reciprocal,
        bottom_known_vector,
        precision=exact_arithmetic_mode,
    )
    leaf_forward = lax.all_gather(forward_portion, "cols", axis=1, tiled=True)
    inverse_full = lax.all_gather(bottom_pivot_reciprocal, "cols", axis=1, tiled=True)
    blocks = leaf_blocks[:, 0]
    targets = leaf_target[:, 0]
    contrib = jnp.einsum("lab,lbr->lar", blocks, leaf_forward, precision=exact_arithmetic_mode)
    top_ids = jnp.arange(row_count, dtype=jnp.int32)
    picker = (targets[:, None] == top_ids[None, :]).astype(jnp.float32)
    top_rows = jnp.arange(1 * lax.axis_size("rows"), dtype=jnp.int32)
    selector = (targets[:, None] == top_rows[None, :]).astype(jnp.float32)
    own_sums = lax.psum_scatter(
        jnp.einsum("lt,lar->tar", selector, contrib, precision=exact_arithmetic_mode),
        "rows",
        scatter_dimension=0,
        tiled=True,
    )
    carried = lax.psum(own_sums, ("cols", "layers"))
    diag_inv = top_inv[0]
    coupling = top_sub[0]
    local_term = jnp.dot(diag_inv, top_rhs[0] - carried[0], precision=exact_arithmetic_mode)
    forward_map = -jnp.dot(diag_inv, coupling, precision=exact_arithmetic_mode)

    def forward_turn(turn_index, current):
        previous = from_behind(current, "rows", 1)
        return local_term + jnp.dot(forward_map, previous, precision=exact_arithmetic_mode)

    top_forward = lax.fori_loop(0, row_count - 1, forward_turn, local_term)
    coupling_next = from_behind(coupling, "rows", -1)
    back_term = jnp.dot(diag_inv.T, top_forward, precision=exact_arithmetic_mode)
    back_map = -jnp.dot(diag_inv.T, coupling_next.T, precision=exact_arithmetic_mode)

    def upward_sweep_pass(turn_index, current):
        following = from_behind(current, "rows", -1)
        return back_term + jnp.dot(back_map, following, precision=exact_arithmetic_mode)

    top_own = lax.fori_loop(0, row_count - 1, upward_sweep_pass, back_term)
    top_part = top_own[None]
    top_all = lax.all_gather(top_part, "rows", axis=0, tiled=True)
    gathered = jnp.einsum("lt,tar->lar", picker, top_all, precision=exact_arithmetic_mode)
    back_part = jnp.einsum("lab,lar->lbr", blocks, gathered, precision=exact_arithmetic_mode)
    back_sum = lax.psum(back_part, "cols")
    leftover_rows = leaf_forward - back_sum
    column_list = lax.dynamic_slice_in_dim(
        inverse_full, lax.axis_index("cols") * distribute_equations, distribute_equations, 2
    )
    leaf_portion = jnp.einsum(
        "edv,edg->evg", column_list, leftover_rows, precision=exact_arithmetic_mode
    )
    return (leaf_portion, top_part)


def solution(mesh):
    in_specs = (
        P(("rows", "layers"), None, None),
        P(("rows", "layers"), "cols", None),
        P(("rows", "layers"), "cols", None, None),
        P(("rows", "layers"), "cols"),
        P("rows", None, None),
        P("rows", None, None),
        P("rows", None, None),
    )
    out_specs = (P(("rows", "layers"), "cols", None), P("rows", None, None))
    return jax.shard_map(
        on_device, mesh=mesh, in_specs=in_specs, out_specs=out_specs, check_vma=False
    )
```

profile of v0, /device:TPU:1, one launch (start us, length us, event | category | flops | bytes accessed | tf_op | source)
XLA Modules:
  0.0 255.4 jit_solution(15227531689109715637)
XLA Ops:
  7.2 1.4 copy-done
  8.6 2.9 %fusion.28 = f32[12,64,256]{2,1,0:T(8,128)} fusion(f32[12,64,128]{2,1,0:T(8,128)} %param.12, f32[12,128,256]{2,1,0:T(8,128)S(1)} %copy-done), kind=kOutput, calls=%fused_computation.31 | convolution fusion | flops 301989888 | bytes 2752512 | tf_op jit(solution)/shard_map/bxr,brl->bxl/dot_general | solution.py:25
  11.5 29.4 %all-gather.3.cloned.1.call-done = f32[12,128,256]{2,1,0:T(8,128)} async-done(((f32[12,64,256]{2,1,0:T(8,128)}), f32[12,128,256]{2,1,0:T(8,128)}) %all-gather.3.cloned.1.call-update) | async-done | bytes 1572880 | tf_op jit(solution)/shard_map/all_gather | solution.py:31
  40.9 4.5 %fusion.10 = f32[12,256,128]{2,1,0:T(8,128)S(1)} fusion(f32[12,128,256]{2,1,0:T(8,128)} %all-gather.3.cloned.1.call-done, f32[12,1,128,128]{3,2,1,0:T(8,128)} %param.13), kind=kOutput, calls=%fused_computation.14 | convolution fusion | flops 603979776 | bytes 3932160 | tf_op jit(solution)/shard_map/lab,lbr->lar/dot_general | solution.py:35
  45.4 1.9 copy.17
  47.3 2.4 fusion
  52.3 18.5 %reduce-scatter.2.cloned.1.call-done = f32[1,128,256]{2,1,0:T(8,128)} async-done(((f32[4,128,256]{2,1,0:T(8,128)}), f32[1,128,256]{2,1,0:T(8,128)}) %reduce-scatter.2.cloned.1.call-update) | async-done | bytes 131088 | tf_op jit(solution)/shard_map/reduce_scatter | solution.py:40
  71.2 54.8 %all-reduce.3.cloned.1.call-done = f32[1,128,256]{2,1,0:T(8,128)} async-done(((f32[1,128,256]{2,1,0:T(8,128)}), f32[1,128,256]{2,1,0:T(8,128)}) %all-reduce.3.cloned.1.call-update) | async-done | bytes 131088 | tf_op jit(solution)/shard_map/psum | solution.py:46
  127.2 17.3 %while.20 = (s32[]{:T(128)}, f32[128,256]{1,0:T(8,128)S(1)}, f32[128,128]{1,0:T(8,128)S(1)}, f32[128,256]{1,0:T(8,128)S(1)}, s32[]{:T(128)}) while((s32[]{:T(128)}, f32[128,256]{1,0:T(8,128)S(1)}, f32[128,128]{1,0:T(8,128)S(1)}, f32[128,256]{1,0:T(8,128)S(1)}, s32[]{:T(128)}) %tuple.37), condition=%wide.region_3.0_spmd, body=%wide.region_2.0_spmd.sunk | while | flops 50364416 | bytes 983141 | solution.py:56
  127.2 3.1 %collective-permute-start = (f32[128,256]{1,0:T(8,128)S(1)}, f32[128,256]{1,0:T(8,128)S(1)}, u32[]{:S(2)}, u32[]{:S(2)}) collective-permute-start(f32[128,256]{1,0:T(8,128)S(1)} %get-tuple-element.128), channel_id=1, source_target_pairs={{0,8},{8,16},{16,24},{1,9},{9,17},{17,25},{2,10},{10,18},{18,26},{... | collective-permute-start | bytes 393224 | tf_op jit(solution)/shard_map/while/body/eval_jaxpr/ppermute | solution.py:10
  130.3 1.9 collective-permute-done
  132.5 3.8 %collective-permute-start = (f32[128,256]{1,0:T(8,128)S(1)}, f32[128,256]{1,0:T(8,128)S(1)}, u32[]{:S(2)}, u32[]{:S(2)}) collective-permute-start(f32[128,256]{1,0:T(8,128)S(1)} %get-tuple-element.128), channel_id=1, source_target_pairs={{0,8},{8,16},{16,24},{1,9},{9,17},{17,25},{2,10},{10,18},{18,26},{... | collective-permute-start | bytes 393224 | tf_op jit(solution)/shard_map/while/body/eval_jaxpr/ppermute | solution.py:10
  136.3 1.9 collective-permute-done
  138.5 3.8 %collective-permute-start = (f32[128,256]{1,0:T(8,128)S(1)}, f32[128,256]{1,0:T(8,128)S(1)}, u32[]{:S(2)}, u32[]{:S(2)}) collective-permute-start(f32[128,256]{1,0:T(8,128)S(1)} %get-tuple-element.128), channel_id=1, source_target_pairs={{0,8},{8,16},{16,24},{1,9},{9,17},{17,25},{2,10},{10,18},{18,26},{... | collective-permute-start | bytes 393224 | tf_op jit(solution)/shard_map/while/body/eval_jaxpr/ppermute | solution.py:10
  142.3 1.9 collective-permute-done
  145.1 20.6 %while.21 = (s32[]{:T(128)}, f32[128,256]{1,0:T(8,128)S(1)}, f32[128,128]{1,0:T(8,128)S(1)}, f32[128,256]{1,0:T(8,128)S(1)}, s32[]{:T(128)}) while((s32[]{:T(128)}, f32[128,256]{1,0:T(8,128)S(1)}, f32[128,128]{1,0:T(8,128)S(1)}, f32[128,256]{1,0:T(8,128)S(1)}, s32[]{:T(128)}) %tuple.40), condition=%wide.region_5.0_spmd, body=%wide.region_4.0_spmd.sunk | while | flops 50364416 | bytes 983141 | solution.py:65
  146.4 4.8 %collective-permute-done.1 = f32[128,256]{1,0:T(8,128)S(1)} collective-permute-done((f32[128,256]{1,0:T(8,128)S(1)}, f32[128,256]{1,0:T(8,128)S(1)}, u32[]{:S(2)}, u32[]{:S(2)}) %collective-permute-start.1) | collective-permute-done | bytes 131104 | tf_op jit(solution)/shard_map/while/body/eval_jaxpr/ppermute | solution.py:10
  152.8 4.9 %collective-permute-done.1 = f32[128,256]{1,0:T(8,128)S(1)} collective-permute-done((f32[128,256]{1,0:T(8,128)S(1)}, f32[128,256]{1,0:T(8,128)S(1)}, u32[]{:S(2)}, u32[]{:S(2)}) %collective-permute-start.1) | collective-permute-done | bytes 131104 | tf_op jit(solution)/shard_map/while/body/eval_jaxpr/ppermute | solution.py:10
  159.3 6.1 %collective-permute-done.1 = f32[128,256]{1,0:T(8,128)S(1)} collective-permute-done((f32[128,256]{1,0:T(8,128)S(1)}, f32[128,256]{1,0:T(8,128)S(1)}, u32[]{:S(2)}, u32[]{:S(2)}) %collective-permute-start.1) | collective-permute-done | bytes 131104 | tf_op jit(solution)/shard_map/while/body/eval_jaxpr/ppermute | solution.py:10
  165.7 12.1 %all-gather = f32[512,256]{1,0:T(8,128)S(1)} all-gather(f32[128,256]{1,0:T(8,128)S(1)} %get-tuple-element.47), channel_id=2, replica_groups=mesh['rows'=4,'cols'=2,'layers'=4] {'rows'}, dimensions={0}, use_global_device_ids=true | all-gather | bytes 655360 | tf_op jit(solution)/shard_map/all_gather | solution.py:67
  179.1 3.7 %fusion.6 = f32[12,128,256]{2,1,0:T(8,128)} fusion(f32[12,128,256]{2,0,1:T(8,128)S(1)} %fusion.13, f32[12,1,128,128]{3,2,1,0:T(8,128)S(1)} %copy-done.2), kind=kOutput, calls=%fused_computation.8 | convolution fusion | flops 603979776 | bytes 3932160 | tf_op jit(solution)/shard_map/lab,lar->lbr/dot_general | solution.py:69
  182.9 7.5 %all_gather.9 = f32[12,128,128]{2,1,0:T(8,128)} all-gather(f32[12,64,128]{2,1,0:T(8,128)S(1)} %copy-done.3), channel_id=1, replica_groups=mesh['rows'=4,'cols'=2,'layers'=4] {'cols'}, dimensions={1}, use_global_device_ids=true | all-gather | bytes 1179648 | tf_op jit(solution)/shard_map/all_gather | solution.py:32
  190.4 54.2 %all-reduce.5.cloned.1.call-done = f32[12,128,256]{2,1,0:T(8,128)} async-done(((f32[12,128,256]{2,1,0:T(8,128)}), f32[12,128,256]{2,1,0:T(8,128)}) %all-reduce.5.cloned.1.call-update) | async-done | bytes 1572880 | tf_op jit(solution)/shard_map/psum | solution.py:70
  244.6 4.3 %fusion.4 = f32[12,64,256]{2,1,0:T(8,128)} fusion(f32[12,128,256]{2,1,0:T(8,128)S(1)} %copy-done.1, f32[12,128,256]{2,1,0:T(8,128)} %all-reduce.5.cloned.1.call-done, f32[12,128,128]{2,1,0:T(8,128)} %all_gather.9, s32[]{:T(128)S(6)} %select_n.3), kind=kOutput, calls=%fused_computation.6 | convolution fusion | flops 302383104 | bytes 4718596 | tf_op jit(solution)/shard_map/edv,edg->evg/dot_general | solution.py:75
  (45 shorter events, 11.4 us)
Async XLA Ops:
  7.2 1.4 copy-start
  7.2 33.7 %all-gather.3.cloned.1.call-start = ((), (), s32[]{:S(2)}) async-start(), calls=%async_computation.1 | async-start | bytes 2359296 | tf_op jit(solution)/shard_map/all_gather | solution.py:31
  11.5 59.3 %reduce-scatter.2.cloned.1.call-start = ((), (), s32[]{:S(2)}) async-start(), calls=%async_computation.2 | async-start | bytes 655360 | tf_op jit(solution)/shard_map/reduce_scatter | solution.py:40
  45.4 2.0 copy-start.8
  47.3 3.4 %copy-start.7 = (f32[1,128,128]{2,1,0:T(8,128)S(1)}, f32[1,128,128]{2,1,0:T(8,128)}, u32[]{:S(2)}) copy-start(f32[1,128,128]{2,1,0:T(8,128)} %param.17) | copy-start | bytes 196612
  47.3 4.7 %copy-start.4 = (f32[1,128,128]{2,1,0:T(8,128)S(1)}, f32[1,128,128]{2,1,0:T(8,128)}, u32[]{:S(2)}) copy-start(f32[1,128,128]{2,1,0:T(8,128)} %param.16) | copy-start | bytes 196612
  49.8 76.2 %copy-start.6 = (f32[1,128,256]{2,1,0:T(8,128)S(1)}, f32[1,128,256]{2,1,0:T(8,128)}, u32[]{:S(2)}) copy-start(f32[1,128,256]{2,1,0:T(8,128)} %param.15) | copy-start | bytes 393220
  50.7 75.3 %all-reduce.3.cloned.1.call-start = ((), (), s32[]{:S(2)}) async-start(), calls=%async_computation.3 | async-start | bytes 262144 | tf_op jit(solution)/shard_map/psum | solution.py:46
  50.8 20.1 %collective-permute-start.2 = (f32[128,128]{1,0:T(8,128)S(1)}, f32[128,128]{1,0:T(8,128)S(1)}, u32[]{:S(2)}, u32[]{:S(2)}) collective-permute-start(f32[128,128]{1,0:T(8,128)S(1)} %bitcast.55), channel_id=1, source_target_pairs={{8,0},{16,8},{24,16},{9,1},{17,9},{25,17},{10,2},{18,10},{26,18},{... | collective-permute-start | bytes 196616 | tf_op jit(solution)/shard_map/ppermute | solution.py:10
  70.8 173.8 %all-reduce.5.cloned.1.call-start = ((), (), s32[]{:S(2)}) async-start(), calls=%async_computation.4 | async-start | bytes 3145728 | tf_op jit(solution)/shard_map/psum | solution.py:70
  127.2 5.0 %collective-permute-start = (f32[128,256]{1,0:T(8,128)S(1)}, f32[128,256]{1,0:T(8,128)S(1)}, u32[]{:S(2)}, u32[]{:S(2)}) collective-permute-start(f32[128,256]{1,0:T(8,128)S(1)} %get-tuple-element.128), channel_id=1, source_target_pairs={{0,8},{8,16},{16,24},{1,9},{9,17},{17,25},{2,10},{10,18},{18,26},{... | collective-permute-start | bytes 393224 | tf_op jit(solution)/shard_map/while/body/eval_jaxpr/ppermute | solution.py:10
  132.5 5.7 %collective-permute-start = (f32[128,256]{1,0:T(8,128)S(1)}, f32[128,256]{1,0:T(8,128)S(1)}, u32[]{:S(2)}, u32[]{:S(2)}) collective-permute-start(f32[128,256]{1,0:T(8,128)S(1)} %get-tuple-element.128), channel_id=1, source_target_pairs={{0,8},{8,16},{16,24},{1,9},{9,17},{17,25},{2,10},{10,18},{18,26},{... | collective-permute-start | bytes 393224 | tf_op jit(solution)/shard_map/while/body/eval_jaxpr/ppermute | solution.py:10
  138.5 5.7 %collective-permute-start = (f32[128,256]{1,0:T(8,128)S(1)}, f32[128,256]{1,0:T(8,128)S(1)}, u32[]{:S(2)}, u32[]{:S(2)}) collective-permute-start(f32[128,256]{1,0:T(8,128)S(1)} %get-tuple-element.128), channel_id=1, source_target_pairs={{0,8},{8,16},{16,24},{1,9},{9,17},{17,25},{2,10},{10,18},{18,26},{... | collective-permute-start | bytes 393224 | tf_op jit(solution)/shard_map/while/body/eval_jaxpr/ppermute | solution.py:10
  145.1 6.1 %collective-permute-start.1 = (f32[128,256]{1,0:T(8,128)S(1)}, f32[128,256]{1,0:T(8,128)S(1)}, u32[]{:S(2)}, u32[]{:S(2)}) collective-permute-start(f32[128,256]{1,0:T(8,128)S(1)} %get-tuple-element.143), channel_id=1, source_target_pairs={{8,0},{16,8},{24,16},{9,1},{17,9},{25,17},{10,2},{18,10},{26,18},{... | collective-permute-start | bytes 393224 | tf_op jit(solution)/shard_map/while/body/eval_jaxpr/ppermute | solution.py:10
  151.5 6.2 %collective-permute-start.1 = (f32[128,256]{1,0:T(8,128)S(1)}, f32[128,256]{1,0:T(8,128)S(1)}, u32[]{:S(2)}, u32[]{:S(2)}) collective-permute-start(f32[128,256]{1,0:T(8,128)S(1)} %get-tuple-element.143), channel_id=1, source_target_pairs={{8,0},{16,8},{24,16},{9,1},{17,9},{25,17},{10,2},{18,10},{26,18},{... | collective-permute-start | bytes 393224 | tf_op jit(solution)/shard_map/while/body/eval_jaxpr/ppermute | solution.py:10
  158.0 7.4 %collective-permute-start.1 = (f32[128,256]{1,0:T(8,128)S(1)}, f32[128,256]{1,0:T(8,128)S(1)}, u32[]{:S(2)}, u32[]{:S(2)}) collective-permute-start(f32[128,256]{1,0:T(8,128)S(1)} %get-tuple-element.143), channel_id=1, source_target_pairs={{8,0},{16,8},{24,16},{9,1},{17,9},{25,17},{10,2},{18,10},{26,18},{... | collective-permute-start | bytes 393224 | tf_op jit(solution)/shard_map/while/body/eval_jaxpr/ppermute | solution.py:10
  165.6 13.5 %copy-start.5 = (f32[128,256]{1,0:T(8,128)}, f32[128,256]{1,0:T(8,128)S(1)}, u32[]{:S(2)}) copy-start(f32[128,256]{1,0:T(8,128)S(1)} %get-tuple-element.47) | copy-start | bytes 393220
  165.7 13.5 %copy-start.2 = (f32[12,1,128,128]{3,2,1,0:T(8,128)S(1)}, f32[12,1,128,128]{3,2,1,0:T(8,128)}, u32[]{:S(2)}) copy-start(f32[12,1,128,128]{3,2,1,0:T(8,128)} %param.13) | copy-start | bytes 2359300
  179.1 3.8 %copy-start.3 = (f32[12,64,128]{2,1,0:T(8,128)S(1)}, f32[12,64,128]{2,1,0:T(8,128)}, u32[]{:S(2)}) copy-start(f32[12,64,128]{2,1,0:T(8,128)} %param.12) | copy-start | bytes 1179652
  182.9 61.8 %copy-start.1 = (f32[12,128,256]{2,1,0:T(8,128)S(1)}, f32[12,128,256]{2,1,0:T(8,128)}, u32[]{:S(2)}) copy-start(f32[12,128,256]{2,1,0:T(8,128)} %all-gather.3.cloned.1.call-done) | copy-start | bytes 4718596
Sparse Core Ops, SparseCore 0:
  11.6 29.2 all-gather.2
  50.8 19.9 reduce-scatter.1
  73.8 52.1 all-reduce.2
  183.0 61.5 all-reduce.4
where the time goes:
time: 257 us; the launch traced here: 255 us
  waiting for transfers between devices  179 us (70%)
  matrix products  22.7 us (9%)
  blocking collectives  19.7 us (8%)
  starting transfers between devices  16 us (6%)
  between operations  14 us (5%)
  local copies, waits for them, and re-layouts  4.35 us (2%)
    psum x1, waiting for transfers between devices, on_device(): carried = lax.psum(own_sums, ('cols', 'layers'))  54.8 us
    psum x1, waiting for transfers between devices, on_device(): back_sum = lax.psum(back_part, 'cols')  54.2 us
    all_gather x1, waiting for transfers between devices, on_device(): leaf_forward = lax.all_gather(forward_portion, 'cols', axis=1, tiled=True)  29.4 us
    ppermute x7, waiting for transfers between devices, from_behind(): return lax.ppermute(x, axis, pairs)  21.6 us
    reduce_scatter x1, waiting for transfers between devices, on_device(): lax.psum_scatter(jnp.einsum('lt,lar->tar', selector, contrib, precision=e...  18.5 us
    ppermute x7, starting transfers between devices, from_behind(): return lax.ppermute(x, axis, pairs)  15.8 us
    all_gather x1, blocking collectives, on_device(): top_all = lax.all_gather(top_part, 'rows', axis=0, tiled=True)  12.1 us
    all_gather x1, blocking collectives, on_device(): lax.all_gather(bottom_pivot_reciprocal, 'cols', axis=1, tiled=True)  7.54 us
  transfers between devices with their start and end apart: 11, of which 10 were waited for; matrix products, arithmetic and copies ran while one was open for 0% of the time, Pallas kernels for 0%

commit v1 on v0

v1 whole, which is shorter than its diff:
```python
import functools

import jax
import jax.numpy as jnp
from jax import lax
from jax.experimental import pallas as pl
from jax.experimental.pallas import tpu as pltpu
from jax.sharding import PartitionSpec as P

F32 = jnp.float32
BF16 = jnp.bfloat16
MESH = pl.DeviceIdType.MESH
LANES = 128


def split(x):
    high = x.astype(BF16)
    low = (x - high.astype(F32)).astype(BF16)
    return high, low


def mul(a, b, rhs_transposed=False):
    (a_high, a_low), (b_high, b_low) = a, b
    axis = 1 if rhs_transposed else 0
    dot = functools.partial(
        lax.dot_general,
        dimension_numbers=(((1,), (axis,)), ((), ())),
        preferred_element_type=F32,
    )
    both = dot(
        jnp.concatenate([a_high, a_low], axis=1), jnp.concatenate([b_high, b_high], axis=axis)
    )
    return both + dot(a_high, b_low)


def peer_of(axis, stride, size, offset):
    index = lax.axis_index(axis)
    place = lax.rem(lax.div(index, stride), size)
    other = lax.rem(place + offset, size)
    return {axis: index + (other - place) * stride}, place, other


def kernel(
    sizes,
    known,
    pivot,
    blocks,
    target,
    top_rhs,
    top_inv,
    top_sub,
    out,
    top_out,
    pivot_full,
    pivot_turned,
    product,
    products,
    targets,
    inv_all,
    sub_all,
    forward_map,
    back_map,
    weights_high,
    weights_low,
    acc,
    full,
    sol,
    *rest,
):
    stages, chunks = sizes
    n_stage = len(stages)
    recv = rest[:n_stage]
    (pivot_sems, product_sems, target_sems, top_sems, sol_sems) = rest[n_stage : n_stage + 5]
    rs_sems = rest[n_stage + 5 : 2 * n_stage + 5]
    ag_sems = rest[2 * n_stage + 5 :]

    n_leaf, b, r = known.shape
    part = pivot.shape[1]
    n_cols = lax.axis_size("cols")
    n_rows = lax.axis_size("rows")
    halves = r // LANES
    col = lax.axis_index("cols")
    row = lax.axis_index("rows")
    layer = lax.axis_index("layers")
    per = n_leaf // chunks
    own_rows = pl.multiple_of(col * part, part)
    sent = []

    barrier = pltpu.get_barrier_semaphore()
    greeted = 0
    for axis, stride, size in stages:
        for offset in range(1, size):
            peer, _, _ = peer_of(axis, stride, size, offset)
            pl.semaphore_signal(barrier, inc=1, device_id=peer, device_id_type=MESH)
            greeted += 1
    pl.semaphore_wait(barrier, greeted)

    def remote(src, dst, sems, slot, peer):
        return pltpu.make_async_remote_copy(
            src_ref=src,
            dst_ref=dst,
            send_sem=sems.at[(0, *slot)],
            recv_sem=sems.at[(1, *slot)],
            device_id=peer,
            device_id_type=MESH,
        )

    def pivot_copy(offset, chunk):
        peer, _, _ = peer_of("cols", 1, n_cols, offset)
        leaves = pl.ds(chunk * per, per)
        return remote(
            pivot.at[leaves],
            pivot_full.at[leaves, pl.ds(own_rows, part), :],
            pivot_sems,
            (offset - 1, chunk),
            peer,
        )

    for chunk in range(chunks):
        for offset in range(1, n_cols):
            copy = pivot_copy(offset, chunk)
            copy.start()
            sent.append(copy)

    target_copies = []
    for offset in range(1, n_cols):
        peer, _, _ = peer_of("cols", 1, n_cols, offset)
        copy = remote(target, targets.at[col], target_sems, (offset - 1,), peer)
        copy.start()
        target_copies.append(copy)
    sent += target_copies

    top_copies = []
    for offset in range(1, n_rows):
        peer, _, _ = peer_of("rows", 1, n_rows, offset)
        for which, (src, dst) in enumerate(((top_inv, inv_all), (top_sub, sub_all))):
            copy = remote(src.at[0], dst.at[row], top_sems, (which, offset - 1), peer)
            copy.start()
            top_copies.append(copy)
    sent += top_copies

    inv_all[row] = top_inv[0]
    sub_all[row] = top_sub[0]
    targets[col] = target[...]

    n_top = n_rows
    per_half = n_top * b
    first = jnp.logical_and(col == 0, layer == 0)
    for h in range(halves):
        for t in range(n_top):
            mine = jnp.logical_and(first, row == t).astype(F32)
            acc[pl.ds(h * per_half + t * b, b), :] = (
                top_rhs[0, :, h * LANES : (h + 1) * LANES] * mine
            )

    def leaf_work(leaf):
        pivot_full[leaf, pl.ds(own_rows, part), :] = pivot[leaf]
        whole = pivot_full[leaf]
        rhs = split(known[leaf])
        block = split(blocks[leaf, 0])
        solved = split(mul(split(whole), rhs))
        contrib = mul(block, solved)
        which = target[pl.ds(leaf, 1), :]
        for t in range(n_top):
            mask = jnp.broadcast_to(which == t, (b, LANES))
            for h in range(halves):
                rows = pl.ds(h * per_half + t * b, b)
                acc[rows, :] = acc[rows, :] - jnp.where(
                    mask, contrib[:, h * LANES : (h + 1) * LANES], 0.0
                )
        turned = whole.T
        pivot_turned[leaf] = turned
        product[leaf] = mul(split(turned), block, rhs_transposed=True)
        out[leaf] = mul(split(pivot_turned[leaf, pl.ds(own_rows, part), :]), solved)

    def chunk_work(chunk, carry):
        for offset in range(1, n_cols):
            pivot_copy(offset, chunk).wait_recv()
        for i in range(per):
            leaf_work(chunk * per + i)
        return carry

    lax.fori_loop(0, chunks, chunk_work, 0)

    starts = [0]
    spans = [acc.shape[0]]

    def share(stage):
        return pl.ds(pl.multiple_of(starts[stage], 8), spans[stage])

    def reduce_start(stage):
        axis, stride, size = stages[stage]
        span = spans[-1] // size
        copies = []
        place = None
        for offset in range(1, size):
            peer, place, other = peer_of(axis, stride, size, offset)
            source = pl.ds(pl.multiple_of(starts[-1] + other * span, 8), span)
            copy = remote(
                acc.at[source], recv[stage].at[offset - 1], rs_sems[stage], (offset - 1,), peer
            )
            copy.start()
            copies.append(copy)
        if place is not None:
            starts.append(starts[-1] + place * span)
        else:
            starts.append(starts[-1])
        spans.append(span)
        return copies

    def reduce_end(stage, copies):
        rows = share(stage + 1)
        total = acc[rows, :]
        for i, copy in enumerate(copies):
            copy.wait_recv()
            total = total + recv[stage][i]
        if stage == n_stage - 1:
            full[rows, :] = total
        else:
            acc[rows, :] = total
        sent.extend(copies)

    def gather_start(buffer, stage, sems):
        axis, stride, size = stages[stage]
        rows = share(stage + 1)
        copies = []
        for offset in range(1, size):
            peer, _, _ = peer_of(axis, stride, size, offset)
            copy = remote(buffer.at[rows], buffer.at[rows], sems, (offset - 1,), peer)
            copy.start()
            copies.append(copy)
        return copies

    def landed(copies):
        for copy in copies:
            copy.wait_recv()
        sent.extend(copies)

    for stage in (0, 1):
        reduce_end(stage, reduce_start(stage))

    product_copies = []
    for offset in range(1, n_cols):
        peer, _, other = peer_of("cols", 1, n_cols, offset)
        rows = pl.ds(pl.multiple_of(other * part, part), part)
        copy = remote(
            product.at[:, rows, :], products.at[col], product_sems, (offset - 1,), peer
        )
        copy.start()
        product_copies.append(copy)

    copies = reduce_start(2)
    for copy in top_copies:
        copy.wait_recv()
    for t in range(n_top):
        inv = inv_all[t]
        if t > 0:
            forward_map[t] = -mul(split(inv), split(sub_all[t]))
        if t < n_top - 1:
            back_map[t] = -mul(split(inv.T), split(sub_all[t + 1]), rhs_transposed=True)
    reduce_end(2, copies)

    reduce_end(3, reduce_start(3))
    landed(gather_start(full, 3, ag_sems[3]))
    copies = gather_start(full, 2, ag_sems[2])
    landed(copies)
    copies = gather_start(full, 1, ag_sems[1])

    for copy in product_copies + target_copies:
        copy.wait_recv()
    sent += product_copies
    products[col] = product[:, pl.ds(own_rows, part), :]

    def weigh(leaf, carry):
        rows = pl.ds(pl.multiple_of(leaf * part, part), part)
        for t in range(n_top):
            value = jnp.zeros((part, b), F32)
            for c in range(n_cols):
                mask = jnp.broadcast_to(targets[c, pl.ds(leaf, 1), :] == t, (part, b))
                value = jnp.where(mask, -products[c, leaf], value)
            high, low = split(value)
            weights_high[rows, t * b : (t + 1) * b] = high
            weights_low[rows, t * b : (t + 1) * b] = low
        return carry

    lax.fori_loop(0, n_leaf, weigh, 0)
    landed(copies)

    own = pl.multiple_of(starts[1], 8)

    def rows_of(t):
        return pl.ds(pl.multiple_of(own + t * b, 8), b)

    current = None
    ahead = []
    for t in range(n_top):
        local = mul(split(inv_all[t]), split(full[rows_of(t), :]))
        if t > 0:
            local = local + mul(split(forward_map[t]), split(current))
        current = local
        ahead.append(mul(split(inv_all[t].T), split(current)))
    current = None
    for t in reversed(range(n_top)):
        value = ahead[t]
        if t < n_top - 1:
            value = value + mul(split(back_map[t]), split(current))
        current = value
        sol[rows_of(t), :] = value
    copies = gather_start(sol, 0, sol_sems)

    def finish(half):
        start = pl.multiple_of(half * per_half, 8)
        high, low = split(sol[pl.ds(start, per_half), :])
        lanes = pl.ds(pl.multiple_of(half * LANES, LANES), LANES)
        for leaf in range(0, n_leaf, 4):
            rows = slice(leaf * part, (leaf + 4) * part)
            dot = functools.partial(jnp.dot, preferred_element_type=F32)
            w_high, w_low = weights_high[rows, :], weights_low[rows, :]
            update = dot(w_high, high) + dot(w_low, high) + dot(w_high, low)
            for i in range(4):
                out[leaf + i, :, lanes] = (
                    out[leaf + i, :, lanes] + update[i * part : (i + 1) * part]
                )
        mine = pl.ds(pl.multiple_of(start + row * b, 8), b)
        top_out[0, :, lanes] = sol[mine, :]

    own_half = lax.rem(layer, 2)
    finish(own_half)
    landed(copies)
    finish(1 - own_half)

    for copy in sent:
        copy.wait_send()


def on_device(known, pivot, blocks, leaf_target, top_rhs, top_inv, top_sub):
    n_leaf, b, r = known.shape
    part = pivot.shape[1]
    n_rows, n_cols, n_layers = (lax.axis_size(a) for a in ("rows", "cols", "layers"))
    n_top = n_rows
    halves = r // LANES
    stages = (
        ("layers", 1, 2),
        ("cols", 1, n_cols),
        ("layers", 2, n_layers // 2),
        ("rows", 1, n_rows),
    )
    chunks = 4
    padded = -(-n_leaf // 8) * 8
    target = jnp.broadcast_to(
        jnp.pad(leaf_target, ((0, padded - n_leaf), (0, 0))), (padded, LANES)
    )
    total = halves * n_top * b
    spans = []
    span = total
    for _, _, size in stages:
        span //= size
        spans.append(span)
    dma = pltpu.SemaphoreType.DMA
    peers = [max(size - 1, 1) for _, _, size in stages]
    vmem = pl.BlockSpec(memory_space=pltpu.VMEM)
    return pl.pallas_call(
        functools.partial(kernel, (stages, chunks)),
        out_shape=(
            jax.ShapeDtypeStruct((n_leaf, part, r), F32),
            jax.ShapeDtypeStruct((1, b, r), F32),
        ),
        in_specs=[vmem] * 7,
        out_specs=(vmem, vmem),
        scratch_shapes=[
            pltpu.VMEM((n_leaf, b, b), F32),
            pltpu.VMEM((n_leaf, b, b), F32),
            pltpu.VMEM((n_leaf, b, b), F32),
            pltpu.VMEM((n_cols, n_leaf, part, b), F32),
            pltpu.VMEM((n_cols, padded, LANES), jnp.int32),
            pltpu.VMEM((n_top, b, b), F32),
            pltpu.VMEM((n_top, b, b), F32),
            pltpu.VMEM((n_top, b, b), F32),
            pltpu.VMEM((n_top, b, b), F32),
            pltpu.VMEM((n_leaf * part, n_top * b), BF16),
            pltpu.VMEM((n_leaf * part, n_top * b), BF16),
            pltpu.VMEM((total, LANES), F32),
            pltpu.VMEM((total, LANES), F32),
            pltpu.VMEM((total, LANES), F32),
            *[pltpu.VMEM((n, s, LANES), F32) for n, s in zip(peers, spans)],
            dma((2, max(n_cols - 1, 1), chunks)),
            dma((2, max(n_cols - 1, 1))),
            dma((2, max(n_cols - 1, 1))),
            dma((2, 2, max(n_rows - 1, 1))),
            dma((2, 1)),
            *[dma((2, n)) for n in peers],
            *[dma((2, n)) for n in peers],
        ],
        compiler_params=pltpu.CompilerParams(
            collective_id=0, has_side_effects=True, vmem_limit_bytes=48 * 1024 * 1024
        ),
    )(known, pivot, blocks, target, top_rhs, top_inv, top_sub)


def solution(mesh):
    in_specs = (
        P(("rows", "layers"), None, None),
        P(("rows", "layers"), "cols", None),
        P(("rows", "layers"), "cols", None, None),
        P(("rows", "layers"), "cols"),
        P("rows", None, None),
        P("rows", None, None),
        P("rows", None, None),
    )
    out_specs = (P(("rows", "layers"), "cols", None), P("rows", None, None))
    return jax.shard_map(
        on_device, mesh=mesh, in_specs=in_specs, out_specs=out_specs, check_vma=False
    )
```

time: 257 us -> 53.1 us (0.21)
  waiting for transfers between devices: 179 us -> 0 us
  Pallas kernels: 0 us -> 43.7 us
  matrix products: 22.7 us -> 0 us
  blocking collectives: 19.7 us -> 0 us
  starting transfers between devices: 16 us -> 0 us
  between operations: 14 us -> 0.65 us
  local copies, waits for them, and re-layouts: 4.35 us -> 8.39 us
    psum x2 -> x0, waiting for transfers between devices: 109 us -> none  [the longest x1 54.8 us: on_device(): carried = lax.psum(own_sums, ('cols', 'layers'))]
    pallas_call x0 -> x1, Pallas kernels: none -> 43.7 us  [on_device(): pl.pallas_call(functools.partial(kernel, (stages, chunks)), out_shape=(ja...]
    all_gather x1 -> x0, waiting for transfers between devices: 29.4 us -> none  [on_device(): leaf_forward = lax.all_gather(forward_portion, 'cols', axis=1, tiled=True)]
    dot_general x16 -> x0, matrix products: 22.7 us -> none  [the longest x1 4.45 us: on_device(): jnp.einsum('lab,lbr->lar', blocks, leaf_forward, precision=exact_arithmet...]
    ppermute x7 -> x0, waiting for transfers between devices: 21.6 us -> none  [from_behind(): return lax.ppermute(x, axis, pairs)]
    all_gather x2 -> x0, blocking collectives: 19.7 us -> none  [the longest x1 12.1 us: on_device(): top_all = lax.all_gather(top_part, 'rows', axis=0, tiled=True)]
    reduce_scatter x1 -> x0, waiting for transfers between devices: 18.5 us -> none  [on_device(): lax.psum_scatter(jnp.einsum('lt,lar->tar', selector, contrib, precision=e...]
    ppermute x7 -> x0, starting transfers between devices: 15.8 us -> none  [from_behind(): return lax.ppermute(x, axis, pairs)]
  transfers between devices with their start and end apart: 11 -> 0, of which waited for: 10 -> 0; matrix products, arithmetic and copies ran while one was open for 0% -> 0% of each run, Pallas kernels for 0% -> 0%
where the time goes in v1:
time: 53.1 us; the launch traced here: 52.8 us
  Pallas kernels  43.7 us (82%)
  local copies, waits for them, and re-layouts  8.39 us (16%)
  between operations  0.65 us (1%)
    pallas_call x1, Pallas kernels, on_device(): pl.pallas_call(functools.partial(kernel, (stages, chunks)), out_shape=(ja...  43.7 us
    unnamed x14, local copies, waits for them, and re-layouts  7.66 us

profile of v1, /device:TPU:1, one launch (start us, length us, event | category | flops | bytes accessed | tf_op | source)
XLA Modules:
  0.0 52.8 jit_solution(9081064874182274070)
XLA Ops:
  0.6 0.7 %pad_bitcast_fusion = s32[16]{0:T(128)S(1)} fusion(s32[12,1]{0,1:T(1,128)} %param.10), kind=kLoop, calls=%fused_computation | loop fusion | bytes 112 | tf_op jit(solution)/shard_map/broadcast_in_dim | solution.py:350
  1.3 0.1 broadcast_in_dim.8.target
  1.4 0.0 copy-start
  1.4 1.4 %copy-done = f32[12,128,256]{2,1,0:T(8,128)S(1)} copy-done((f32[12,128,256]{2,1,0:T(8,128)S(1)}, f32[12,128,256]{2,1,0:T(8,128)}, u32[]{:S(2)}) %copy-start) | copy-done | bytes 1572888
  2.8 0.0 copy-start.1
  2.8 1.1 %copy-done.1 = f32[12,1,128,128]{3,2,1,0:T(8,128)S(1)} copy-done((f32[12,1,128,128]{3,2,1,0:T(8,128)S(1)}, f32[12,1,128,128]{3,2,1,0:T(8,128)}, u32[]{:S(2)}) %copy-start.1) | copy-done | bytes 786456
  3.9 0.0 copy-start.2
  3.9 1.0 %copy-done.2 = f32[12,64,128]{2,1,0:T(8,128)S(1)} copy-done((f32[12,64,128]{2,1,0:T(8,128)S(1)}, f32[12,64,128]{2,1,0:T(8,128)}, u32[]{:S(2)}) %copy-start.2) | copy-done | bytes 393240
  4.9 0.0 copy-start.3
  4.9 0.9 %copy-done.3 = f32[1,128,256]{2,1,0:T(8,128)S(1)} copy-done((f32[1,128,256]{2,1,0:T(8,128)S(1)}, f32[1,128,256]{2,1,0:T(8,128)}, u32[]{:S(2)}) %copy-start.3) | copy-done | bytes 131096
  5.8 0.0 copy-start.4
  5.8 0.8 %copy-done.4 = f32[1,128,128]{2,1,0:T(8,128)S(1)} copy-done((f32[1,128,128]{2,1,0:T(8,128)S(1)}, f32[1,128,128]{2,1,0:T(8,128)}, u32[]{:S(2)}) %copy-start.4) | copy-done | bytes 65560
  6.6 0.0 copy-start.5
  6.6 0.8 %copy-done.5 = f32[1,128,128]{2,1,0:T(8,128)S(1)} copy-done((f32[1,128,128]{2,1,0:T(8,128)S(1)}, f32[1,128,128]{2,1,0:T(8,128)}, u32[]{:S(2)}) %copy-start.5) | copy-done | bytes 65560
  7.5 43.7 %shard_map.86 = (f32[12,64,256]{2,1,0:T(8,128)S(1)}, f32[1,128,256]{2,1,0:T(8,128)S(1)}) custom-call(f32[12,128,256]{2,1,0:T(8,128)S(1)} %copy-done, f32[12,64,128]{2,1,0:T(8,128)S(1)} %copy-done.2, f32[12,1,128,128]{3,2,1,0:T(8,128)S(1)} %copy-done.1, s32[16,128]{1,0:T(8,128)S(1)} %broadcast_in_dim.8.target, f32[1,128,256]{2,1,0:T(8,128)S(1)} %copy-done.3, ...), custom_call_target="tpu_custom_call" | custom-call | tf_op jit(solution)/shard_map/pallas_call | solution.py:362
  51.2 0.9 %copy.11 = f32[12,64,256]{2,1,0:T(8,128)} copy(f32[12,64,256]{2,1,0:T(8,128)S(1)} %get-tuple-element.4) | data formatting | bytes 1572864
  52.1 0.7 %copy.12 = f32[1,128,256]{2,1,0:T(8,128)} copy(f32[1,128,256]{2,1,0:T(8,128)S(1)} %get-tuple-element.5) | data formatting | bytes 262144
Async XLA Ops:
  1.4 1.4 %copy-start = (f32[12,128,256]{2,1,0:T(8,128)S(1)}, f32[12,128,256]{2,1,0:T(8,128)}, u32[]{:S(2)}) copy-start(f32[12,128,256]{2,1,0:T(8,128)} %known.1) | copy-start | bytes 4718596
  2.8 1.1 %copy-start.1 = (f32[12,1,128,128]{3,2,1,0:T(8,128)S(1)}, f32[12,1,128,128]{3,2,1,0:T(8,128)}, u32[]{:S(2)}) copy-start(f32[12,1,128,128]{3,2,1,0:T(8,128)} %blocks.1) | copy-start | bytes 2359300
  3.9 1.0 %copy-start.2 = (f32[12,64,128]{2,1,0:T(8,128)S(1)}, f32[12,64,128]{2,1,0:T(8,128)}, u32[]{:S(2)}) copy-start(f32[12,64,128]{2,1,0:T(8,128)} %pivot.1) | copy-start | bytes 1179652
  4.9 0.9 %copy-start.3 = (f32[1,128,256]{2,1,0:T(8,128)S(1)}, f32[1,128,256]{2,1,0:T(8,128)}, u32[]{:S(2)}) copy-start(f32[1,128,256]{2,1,0:T(8,128)} %top_rhs.1) | copy-start | bytes 393220
  5.8 0.8 %copy-start.4 = (f32[1,128,128]{2,1,0:T(8,128)S(1)}, f32[1,128,128]{2,1,0:T(8,128)}, u32[]{:S(2)}) copy-start(f32[1,128,128]{2,1,0:T(8,128)} %top_inv.1) | copy-start | bytes 196612
  6.6 0.8 %copy-start.5 = (f32[1,128,128]{2,1,0:T(8,128)S(1)}, f32[1,128,128]{2,1,0:T(8,128)}, u32[]{:S(2)}) copy-start(f32[1,128,128]{2,1,0:T(8,128)} %top_sub.1) | copy-start | bytes 196612

commit v2 on v1

v2 whole, which is shorter than its diff:
```python
import functools

import jax
import jax.numpy as jnp
from jax import lax
from jax.experimental import pallas as pl
from jax.experimental.pallas import tpu as pltpu
from jax.sharding import PartitionSpec as P

F32 = jnp.float32
BF16 = jnp.bfloat16
MESH = pl.DeviceIdType.MESH
LANES = 128


def split(x):
    high = x.astype(BF16)
    low = (x - high.astype(F32)).astype(BF16)
    return high, low


def mul(a, b, rhs_transposed=False):
    (a_high, a_low), (b_high, b_low) = a, b
    axis = 1 if rhs_transposed else 0
    dot = functools.partial(
        lax.dot_general,
        dimension_numbers=(((1,), (axis,)), ((), ())),
        preferred_element_type=F32,
    )
    if a_high.shape[1] > 128:
        return dot(a_high, b_high) + dot(a_low, b_high) + dot(a_high, b_low)
    both = dot(
        jnp.concatenate([a_high, a_low], axis=1), jnp.concatenate([b_high, b_high], axis=axis)
    )
    return both + dot(a_high, b_low)


def group_size(stage):
    total = 1
    for _, _, size in stage:
        total *= size
    return total


def peer_of(stage, offset):
    device, place, other = {}, 0, 0
    for axis, stride, size in stage:
        offset, digit = divmod(offset, size)
        index = lax.axis_index(axis)
        mine = lax.rem(lax.div(index, stride), size)
        theirs = lax.rem(mine + digit, size)
        if size > 1:
            device[axis] = index + (theirs - mine) * stride
        place = place * size + mine
        other = other * size + theirs
    return device, place, other


def kernel(
    sizes,
    known_hbm,
    pivot,
    blocks_hbm,
    target_smem,
    rhs_hbm,
    top_inv,
    top_sub,
    out,
    top_out,
    known,
    blocks,
    target,
    top_rhs,
    pivot_full,
    pivot_turned,
    solved_high,
    solved_low,
    product,
    products,
    targets,
    inv_all,
    sub_all,
    forward_map,
    back_map,
    lower_high,
    lower_low,
    inverse_high,
    inverse_low,
    weights_high,
    weights_low,
    acc,
    full,
    sol,
    *rest,
):
    stages, chunks = sizes
    n_stage = len(stages)
    recv = rest[:n_stage]
    (local_sems, pivot_sems, product_sems, target_sems, top_sems, sol_sems) = rest[
        n_stage : n_stage + 6
    ]
    rs_sems = rest[n_stage + 6 : 2 * n_stage + 6]
    ag_sems = rest[2 * n_stage + 6 :]

    n_leaf, b, r = known.shape
    part = pivot.shape[1]
    n_cols = lax.axis_size("cols")
    n_rows = lax.axis_size("rows")
    n_top = n_rows
    halves = r // LANES
    col = lax.axis_index("cols")
    row = lax.axis_index("rows")
    layer = lax.axis_index("layers")
    per = n_leaf // chunks
    own_rows = pl.multiple_of(col * part, part)
    cols_stage = (("cols", 1, n_cols),)
    rows_stage = (("rows", 1, n_rows),)
    sent = []

    barrier = pltpu.get_barrier_semaphore()
    greeted = 0
    for stage in stages:
        for offset in range(1, group_size(stage)):
            peer, _, _ = peer_of(stage, offset)
            pl.semaphore_signal(barrier, inc=1, device_id=peer, device_id_type=MESH)
            greeted += 1

    loads = [
        pltpu.make_async_copy(src, dst, local_sems.at[i])
        for i, (src, dst) in enumerate(
            (
                (pivot, pivot_full.at[:, pl.ds(own_rows, part), :]),
                (known_hbm, known),
                (blocks_hbm.at[:, 0], blocks),
                (rhs_hbm.at[0], top_rhs),
                (top_inv.at[0], inv_all.at[row]),
                (top_sub.at[0], sub_all.at[row]),
            )
        )
    ]
    for copy in loads:
        copy.start()
    for leaf in range(n_leaf):
        target[leaf : leaf + 1, :] = jnp.full((1, LANES), target_smem[leaf, 0], jnp.int32)
    for leaf in range(n_leaf, target.shape[0]):
        target[leaf : leaf + 1, :] = jnp.zeros((1, LANES), jnp.int32)
    targets[col] = target[...]
    pl.semaphore_wait(barrier, greeted)

    def remote(src, dst, sems, slot, peer):
        return pltpu.make_async_remote_copy(
            src_ref=src,
            dst_ref=dst,
            send_sem=sems.at[(0, *slot)],
            recv_sem=sems.at[(1, *slot)],
            device_id=peer,
            device_id_type=MESH,
        )

    def pivot_copy(offset, chunk):
        peer, _, _ = peer_of(cols_stage, offset)
        leaves = pl.ds(chunk * per, per)
        return remote(
            pivot.at[leaves],
            pivot_full.at[leaves, pl.ds(own_rows, part), :],
            pivot_sems,
            (offset - 1, chunk),
            peer,
        )

    for chunk in range(chunks):
        for offset in range(1, n_cols):
            copy = pivot_copy(offset, chunk)
            copy.start()
            sent.append(copy)

    target_copies = []
    for offset in range(1, n_cols):
        peer, _, _ = peer_of(cols_stage, offset)
        copy = remote(target, targets.at[col], target_sems, (offset - 1,), peer)
        copy.start()
        target_copies.append(copy)
    sent += target_copies

    top_copies = []
    for offset in range(1, n_rows):
        peer, _, _ = peer_of(rows_stage, offset)
        for which, (src, dst) in enumerate(((top_inv, inv_all), (top_sub, sub_all))):
            copy = remote(src.at[0], dst.at[row], top_sems, (which, offset - 1), peer)
            copy.start()
            top_copies.append(copy)
    sent += top_copies

    for copy in loads:
        copy.wait()

    per_half = n_top * b
    first = jnp.logical_and(col == 0, layer == 0)
    for h in range(halves):
        for t in range(n_top):
            mine = jnp.logical_and(first, row == t).astype(F32)
            acc[pl.ds(h * per_half + t * b, b), :] = (
                top_rhs[:, h * LANES : (h + 1) * LANES] * mine
            )

    def forward_work(chunk):
        for offset in range(1, n_cols):
            pivot_copy(offset, chunk).wait_recv()
        contribs, picks = [], []
        for i in range(per):
            leaf = chunk * per + i
            solved = split(mul(split(pivot_full[leaf]), split(known[leaf])))
            solved_high[i], solved_low[i] = solved
            contribs.append(mul(split(blocks[leaf]), solved))
            picks.append(target[pl.ds(leaf, 1), :])
        for t in range(n_top):
            masks = [jnp.broadcast_to(pick == t, (b, LANES)) for pick in picks]
            for h in range(halves):
                rows = pl.ds(h * per_half + t * b, b)
                total = acc[rows, :]
                for mask, contrib in zip(masks, contribs):
                    total = total - jnp.where(
                        mask, contrib[:, h * LANES : (h + 1) * LANES], 0.0
                    )
                acc[rows, :] = total

    def later_work(chunk):
        for i in range(per):
            leaf = chunk * per + i
            turned = pivot_full[leaf].T
            pivot_turned[leaf] = turned
            product[leaf] = mul(split(turned), split(blocks[leaf]), rhs_transposed=True)
            own = split(pivot_turned[leaf, pl.ds(own_rows, part), :])
            out[leaf] = mul(own, (solved_high[i], solved_low[i]))

    def chunk_work(chunk, carry):
        forward_work(chunk)
        later_work(chunk)
        return carry

    lax.fori_loop(0, chunks - 1, chunk_work, 0)
    forward_work(chunks - 1)

    starts = [0]
    spans = [acc.shape[0]]

    def share(stage):
        return pl.ds(pl.multiple_of(starts[stage], 8), spans[stage])

    def reduce_start(stage):
        size = group_size(stages[stage])
        span = spans[-1] // size
        copies = []
        for offset in range(1, size):
            peer, _, other = peer_of(stages[stage], offset)
            source = pl.ds(pl.multiple_of(starts[-1] + other * span, 8), span)
            copy = remote(
                acc.at[source], recv[stage].at[offset - 1], rs_sems[stage], (offset - 1,), peer
            )
            copy.start()
            copies.append(copy)
        _, place, _ = peer_of(stages[stage], 0)
        starts.append(starts[-1] + place * span)
        spans.append(span)
        return copies

    def reduce_end(stage, copies):
        rows = share(stage + 1)
        total = acc[rows, :]
        for i, copy in enumerate(copies):
            copy.wait_recv()
            total = total + recv[stage][i]
        if stage == n_stage - 1:
            full[rows, :] = total
        else:
            acc[rows, :] = total
        sent.extend(copies)

    def gather_start(buffer, stage, sems):
        rows = share(stage + 1)
        copies = []
        for offset in range(1, group_size(stages[stage])):
            peer, _, _ = peer_of(stages[stage], offset)
            copy = remote(buffer.at[rows], buffer.at[rows], sems, (offset - 1,), peer)
            copy.start()
            copies.append(copy)
        return copies

    def landed(copies):
        for copy in copies:
            copy.wait_recv()
        sent.extend(copies)

    def each(first, last, body):
        if n_top <= 4:
            for t in range(first, last):
                body(t)
        else:
            lax.fori_loop(first, last, lambda t, carry: (body(t), carry)[1], 0)

    def rows_at(t, start=0):
        return pl.ds(pl.multiple_of(start + t * b, 8), b)

    copies = reduce_start(0)
    later_work(chunks - 1)
    reduce_end(0, copies)
    copies = reduce_start(1)

    for copy in top_copies:
        copy.wait_recv()

    def forward_step(t):
        forward_map[t] = -mul(split(inv_all[t]), split(sub_all[t]))

    def back_step(t):
        back_map[t] = -mul(split(inv_all[t].T), split(sub_all[t + 1]), rhs_transposed=True)

    def lower_step(t):
        before = rows_at(t - 1)
        value = mul(split(forward_map[t]), (lower_high[before, :], lower_low[before, :]))
        lower_high[rows_at(t), :], lower_low[rows_at(t), :] = split(value)
        place_inverse(t)

    def place_inverse(t):
        lanes = pl.ds(pl.multiple_of(t * b, b), b)
        high, low = split(inv_all[t])
        lower_high[rows_at(t), lanes] = high
        lower_low[rows_at(t), lanes] = low

    def inverse_step(i):
        t = n_top - 1 - i
        here, after = rows_at(t), rows_at(t + 1)
        value = mul(split(inv_all[t].T), (lower_high[here, :], lower_low[here, :]))
        if not (isinstance(i, int) and i == 0):
            value = value + mul(
                split(back_map[t]), (inverse_high[after, :], inverse_low[after, :])
            )
        inverse_high[here, :], inverse_low[here, :] = split(value)

    each(1, n_top, forward_step)
    each(0, n_top - 1, back_step)
    reduce_end(1, copies)

    product_copies = []
    for offset in range(1, n_cols):
        peer, _, other = peer_of(cols_stage, offset)
        rows = pl.ds(pl.multiple_of(other * part, part), part)
        copy = remote(
            product.at[:, rows, :], products.at[col], product_sems, (offset - 1,), peer
        )
        product_copies.append(copy)

    copies = reduce_start(2)
    for copy in product_copies:
        copy.start()
    lower_high[0:b, :] = jnp.zeros((b, n_top * b), BF16)
    lower_low[0:b, :] = jnp.zeros((b, n_top * b), BF16)
    place_inverse(0)
    each(1, n_top, lower_step)
    reduce_end(2, copies)
    copies = gather_start(full, 2, ag_sems[2])
    inverse_step(0)
    each(1, n_top, inverse_step)
    landed(copies)
    copies = gather_start(full, 1, ag_sems[1])

    for copy in product_copies + target_copies:
        copy.wait_recv()
    sent += product_copies
    products[col] = product[:, pl.ds(own_rows, part), :]

    def weigh(leaf, carry):
        rows = pl.ds(pl.multiple_of(leaf * part, part), part)
        for t in range(n_top):
            value = jnp.zeros((part, b), F32)
            for c in range(n_cols):
                mask = jnp.broadcast_to(targets[c, pl.ds(leaf, 1), :] == t, (part, b))
                value = jnp.where(mask, -products[c, leaf], value)
            high, low = split(value)
            weights_high[rows, t * b : (t + 1) * b] = high
            weights_low[rows, t * b : (t + 1) * b] = low
        return carry

    lax.fori_loop(0, n_leaf, weigh, 0)
    landed(copies)

    own = pl.multiple_of(starts[1], 8)
    right = split(full[pl.ds(own, per_half), :])

    def solve_rows(t):
        here = rows_at(t)
        sol[rows_at(t, own), :] = mul((inverse_high[here, :], inverse_low[here, :]), right)

    each(0, n_top, solve_rows)
    copies = gather_start(sol, 0, sol_sems)

    def finish(half):
        start = pl.multiple_of(half * per_half, 8)
        high, low = split(sol[pl.ds(start, per_half), :])
        lanes = pl.ds(pl.multiple_of(half * LANES, LANES), LANES)
        for leaf in range(0, n_leaf, 4):
            rows = slice(leaf * part, (leaf + 4) * part)
            dot = functools.partial(jnp.dot, preferred_element_type=F32)
            w_high, w_low = weights_high[rows, :], weights_low[rows, :]
            update = dot(w_high, high) + dot(w_low, high) + dot(w_high, low)
            for i in range(4):
                out[leaf + i, :, lanes] = (
                    out[leaf + i, :, lanes] + update[i * part : (i + 1) * part]
                )
        mine = pl.ds(pl.multiple_of(start + row * b, 8), b)
        top_out[0, :, lanes] = sol[mine, :]

    own_half = lax.rem(layer, 2)
    finish(own_half)
    landed(copies)
    finish(1 - own_half)

    for copy in sent:
        copy.wait_send()


def on_device(known, pivot, blocks, leaf_target, top_rhs, top_inv, top_sub):
    n_leaf, b, r = known.shape
    part = pivot.shape[1]
    n_rows, n_cols, n_layers = (lax.axis_size(a) for a in ("rows", "cols", "layers"))
    n_top = n_rows
    halves = r // LANES
    stages = (
        (("layers", 1, 2),),
        (("cols", 1, n_cols), ("layers", 2, n_layers // 2)),
        (("rows", 1, n_rows),),
    )
    chunks = 4
    padded = -(-n_leaf // 8) * 8
    total = halves * n_top * b
    spans = []
    span = total
    for stage in stages:
        span //= group_size(stage)
        spans.append(span)
    dma = pltpu.SemaphoreType.DMA
    peers = [max(group_size(stage) - 1, 1) for stage in stages]
    hbm = pl.BlockSpec(memory_space=pltpu.HBM)
    vmem = pl.BlockSpec(memory_space=pltpu.VMEM)
    return pl.pallas_call(
        functools.partial(kernel, (stages, chunks)),
        out_shape=(
            jax.ShapeDtypeStruct((n_leaf, part, r), F32),
            jax.ShapeDtypeStruct((1, b, r), F32),
        ),
        in_specs=[hbm, hbm, hbm, pl.BlockSpec(memory_space=pltpu.SMEM), hbm, hbm, hbm],
        out_specs=(vmem, vmem),
        scratch_shapes=[
            pltpu.VMEM((n_leaf, b, r), F32),
            pltpu.VMEM((n_leaf, b, b), F32),
            pltpu.VMEM((padded, LANES), jnp.int32),
            pltpu.VMEM((b, r), F32),
            pltpu.VMEM((n_leaf, b, b), F32),
            pltpu.VMEM((n_leaf, b, b), F32),
            pltpu.VMEM((n_leaf // chunks, b, r), BF16),
            pltpu.VMEM((n_leaf // chunks, b, r), BF16),
            pltpu.VMEM((n_leaf, b, b), F32),
            pltpu.VMEM((n_cols, n_leaf, part, b), F32),
            pltpu.VMEM((n_cols, padded, LANES), jnp.int32),
            pltpu.VMEM((n_top, b, b), F32),
            pltpu.VMEM((n_top, b, b), F32),
            pltpu.VMEM((n_top, b, b), F32),
            pltpu.VMEM((n_top, b, b), F32),
            *[pltpu.VMEM((n_top * b, n_top * b), BF16)] * 4,
            pltpu.VMEM((n_leaf * part, n_top * b), BF16),
            pltpu.VMEM((n_leaf * part, n_top * b), BF16),
            pltpu.VMEM((total, LANES), F32),
            pltpu.VMEM((total, LANES), F32),
            pltpu.VMEM((total, LANES), F32),
            *[pltpu.VMEM((n, s, LANES), F32) for n, s in zip(peers, spans)],
            dma((6,)),
            dma((2, max(n_cols - 1, 1), chunks)),
            dma((2, max(n_cols - 1, 1))),
            dma((2, max(n_cols - 1, 1))),
            dma((2, 2, max(n_rows - 1, 1))),
            dma((2, 1)),
            *[dma((2, n)) for n in peers],
            *[dma((2, n)) for n in peers],
        ],
        compiler_params=pltpu.CompilerParams(
            collective_id=0, has_side_effects=True, vmem_limit_bytes=60 * 1024 * 1024
        ),
    )(known, pivot, blocks, leaf_target, top_rhs, top_inv, top_sub)


def solution(mesh):
    in_specs = (
        P(("rows", "layers"), None, None),
        P(("rows", "layers"), "cols", None),
        P(("rows", "layers"), "cols", None, None),
        P(("rows", "layers"), "cols"),
        P("rows", None, None),
        P("rows", None, None),
        P("rows", None, None),
    )
    out_specs = (P(("rows", "layers"), "cols", None), P("rows", None, None))
    return jax.shard_map(
        on_device, mesh=mesh, in_specs=in_specs, out_specs=out_specs, check_vma=False
    )
```

time: 53.1 us -> 45.9 us (0.86)
  local copies, waits for them, and re-layouts: 8.39 us -> 4.09 us
  Pallas kernels: 43.7 us -> 40.9 us
    unnamed x14 -> x5, local copies, waits for them, and re-layouts: 7.66 us -> 4.09 us
    pallas_call x1, Pallas kernels: 43.7 us -> 40.9 us  [on_device(): pl.pallas_call(functools.partial(kernel, (stages, chunks)), out_shape=(ja...]
    broadcast_in_dim x2 -> x0, local copies, waits for them, and re-layouts: 0.73 us -> none  [on_device(): jnp.broadcast_to(jnp.pad(leaf_target, ((0, padded - n_leaf), (0, 0))), (p...]
where the time goes in v2:
time: 45.9 us; the launch traced here: 45.7 us
  Pallas kernels  40.9 us (89%)
  local copies, waits for them, and re-layouts  4.09 us (9%)
  between operations  0.65 us (1%)
    pallas_call x1, Pallas kernels, on_device(): pl.pallas_call(functools.partial(kernel, (stages, chunks)), out_shape=(ja...  40.9 us
    unnamed x5, local copies, waits for them, and re-layouts  4.09 us

profile of v2, /device:TPU:1, one launch (start us, length us, event | category | flops | bytes accessed | tf_op | source)
XLA Modules:
  0.0 45.7 jit_solution(749928017065718278)
XLA Ops:
  0.6 1.3 %copy.9.target_smem = s32[12,1]{1,0:T(8,128)} copy(s32[12,1]{0,1:T(1,128)} %param.10) | data formatting | bytes 96 | tf_op args[3]
  2.0 40.9 %shard_map.86 = (f32[12,64,256]{2,1,0:T(8,128)}, f32[1,128,256]{2,1,0:T(8,128)}) custom-call(f32[12,128,256]{2,1,0:T(8,128)} %known_hbm.1, f32[12,64,128]{2,1,0:T(8,128)} %pivot.1, f32[12,1,128,128]{3,2,1,0:T(8,128)} %blocks_hbm.1, s32[12,1]{1,0:T(8,128)} %copy.9.target_smem, f32[1,128,256]{2,1,0:T(8,128)} %rhs_hbm.1, f32[1,128,128]{2,1,0:T(8,128)} %top_inv.1, ...), custom_call_target="tpu_custom_call" | custom-call | tf_op jit(solution)/shard_map/pallas_call | solution.py:445
  42.9 0.0 copy-start
  42.9 2.1 %copy.12 = f32[12,64,256]{2,1,0:T(8,128)} copy(f32[12,64,256]{2,1,0:T(8,128)} %get-tuple-element.4) | data formatting | bytes 1572864
  45.0 0.0 copy-done
  45.0 0.7 %copy.13 = f32[1,128,256]{2,1,0:T(8,128)} copy(f32[1,128,256]{2,1,0:T(8,128)S(1)} %copy-done) | data formatting | bytes 262144
Async XLA Ops:
  42.9 2.1 %copy-start = (f32[1,128,256]{2,1,0:T(8,128)S(1)}, f32[1,128,256]{2,1,0:T(8,128)}, u32[]{:S(2)}) copy-start(f32[1,128,256]{2,1,0:T(8,128)} %get-tuple-element.5) | copy-start | bytes 393220
